TPU v7x, 256 devices: a whole 4x4x8 slice. The times are simulated.
256 devices in a mesh: prow: 16 (over z, core), pcol: 16 (over x, y).
Axes of the slice: x: 4, y: 4, z: 8, core: 2. Of those that a mesh axis runs over, the one named last changes fastest.
Arguments:
- leaf_source: bfloat16 [16, 16, 8, 256, 128], P('prow', 'pcol'), may hold values from -6 to 6
- band_source: bfloat16 [16, 256, 128], P('prow'), may hold values from -6 to 6
- strip_source: bfloat16 [16, 256, 128], P('pcol'), may hold values from -6 to 6
- summit_source: bfloat16 [256, 128], replicated, may hold values from -6 to 6
- leaf_inverse: bfloat16 [16, 16, 8, 256, 256], P('prow', 'pcol'), may hold values from -1 to 2
- band_inverse: bfloat16 [16, 256, 256], P('prow'), may hold values from -1 to 2
- strip_inverse: bfloat16 [16, 256, 256], P('pcol'), may hold values from -1 to 2
- summit_inverse: bfloat16 [256, 256], replicated, may hold values from -1 to 2
- leaf_blocks: bfloat16 [16, 16, 28, 256, 256], P('prow', 'pcol'), may hold values from -0.09375 to 0.09375
- band_blocks: bfloat16 [16, 16, 8, 256, 256], P('prow', 'pcol'), may hold values from -0.0234375 to 0.0234375
- strip_blocks: bfloat16 [16, 16, 8, 256, 256], P('prow', 'pcol'), may hold values from -0.0234375 to 0.0234375
- summit_blocks: bfloat16 [16, 16, 8, 256, 256], P('prow', 'pcol'), may hold values from -0.015625 to 0.015625
- coupling: bfloat16 [16, 16, 256, 256], P('prow', 'pcol'), may hold values from -0.0625 to 0.0625
- summit_band: bfloat16 [16, 256, 256], P('prow', 'pcol'), may hold values from -0.046875 to 0.046875
- summit_strip: bfloat16 [16, 256, 256], P('pcol'), may hold values from -0.046875 to 0.046875
- parents: int32 [16, 16, 8], P('prow', 'pcol'), may hold values from 1 to 8, as said below
- widths: int32 [16, 16, 8], P('prow', 'pcol'), may hold values from 64 to 256
Outputs:
- leaf_answer: bfloat16 [16, 16, 8, 256, 128], P('prow', 'pcol')
- band_answer: bfloat16 [16, 256, 128], P('prow')
- strip_answer: bfloat16 [16, 256, 128], P('pcol')
- summit_answer: bfloat16 [256, 128], replicated
Inputs may be any that keep to these rules, and one draw needn't show every extreme that they name: parents[r, c, a] is a later leaf of the same subtree, or 8 where leaf a links only to the separators.
All inputs are finite; a program needn't handle non-finite values.
Results may differ from a plain program's by a relative error of at most 0.015.
Values sent between devices are 32-bit elements; how exact they have to be, the bound alone decides.
A program may use at most 64 MiB of HBM per device.

v0:
```python
import jax
import jax.numpy as jnp
from jax import lax
from jax.sharding import PartitionSpec as P

PASSES = 2


def ancestors(parent_list, leaf_count):
    node_ids = jnp.arange(leaf_count + 1, dtype=jnp.int32)
    current = parent_list
    extended = jnp.concatenate([current, jnp.full((1,), leaf_count, jnp.int32)])
    reached = jnp.zeros((leaf_count + 1, leaf_count), jnp.float32)
    for repeat in range(leaf_count):
        matches = current[None, :] == node_ids[:, None]
        reached = jnp.maximum(reached, matches.astype(jnp.float32))
        current = jnp.sum(jnp.where(matches, extended[:, None], 0), axis=0)
    return reached[:leaf_count]


def multiply(left, right, form):
    return jnp.einsum(form, left, right, preferred_element_type=jnp.float32)


def forward_block(inverse, source, partial_value):
    residual = (source.astype(jnp.float32) - partial_value).astype(jnp.bfloat16)
    return multiply(inverse, residual, "ij,jr->ir").astype(jnp.bfloat16)


def backward_block(inverse, source, partial_value):
    residual = (source.astype(jnp.float32) - partial_value).astype(jnp.bfloat16)
    return multiply(inverse, residual, "ji,jr->ir").astype(jnp.bfloat16)


def leaf_forward(pair_blocks, inverses, sources, reached, row_mask):
    leaf_count = sources.shape[0]
    solved = []
    for position in range(leaf_count):
        residual = sources[position].astype(jnp.float32)
        if position > 0:
            first_pair = position * (position - 1) // 2
            weights = reached[position, :position].astype(jnp.bfloat16)
            stacked = jnp.stack(solved) * weights[:, None, None]
            residual = residual - multiply(
                pair_blocks[first_pair : first_pair + position], stacked, "bij,bjr->ir"
            )
        residual = (row_mask[position] * residual).astype(jnp.bfloat16)
        solved.append(
            (row_mask[position] * multiply(inverses[position], residual, "ij,jr->ir")).astype(
                jnp.bfloat16
            )
        )
    return jnp.stack(solved)


def leaf_backward(pair_blocks, inverses, solved, outer, reached, row_mask):
    leaf_count = solved.shape[0]
    pending = outer
    answers = [None] * leaf_count
    for position in reversed(range(leaf_count)):
        residual = (
            row_mask[position] * (solved[position].astype(jnp.float32) - pending[position])
        ).astype(jnp.bfloat16)
        update = (row_mask[position] * multiply(inverses[position], residual, "ji,jr->ir")).astype(
            jnp.bfloat16
        )
        answers[position] = update
        if position > 0:
            first_pair = position * (position - 1) // 2
            pushed = multiply(
                pair_blocks[first_pair : first_pair + position], update, "bji,jr->bir"
            )
            pending = pending.at[:position].add(
                reached[position, :position][:, None, None] * pushed
            )
    return jnp.stack(answers)


def per_device(
    leaf_source,
    band_source,
    strip_source,
    summit_source,
    leaf_inverse,
    band_inverse,
    strip_inverse,
    summit_inverse,
    leaf_blocks,
    band_blocks,
    strip_blocks,
    summit_blocks,
    coupling,
    summit_band,
    summit_strip,
    parents,
    widths,
):
    leaf_count = leaf_source.shape[2]
    block_width = leaf_source.shape[3]
    reached = ancestors(parents[0, 0], leaf_count)
    column_ids = jnp.arange(block_width, dtype=jnp.int32)
    row_mask = (column_ids[None, :] < widths[0, 0][:, None]).astype(jnp.float32)[:, :, None]
    band_slab = summit_band.shape[1]
    strip_slab = block_width // lax.axis_size("prow")
    column_place = lax.axis_index("pcol") * band_slab
    row_place = lax.axis_index("prow") * strip_slab
    inverses = leaf_inverse[0, 0]
    pair_blocks = leaf_blocks[0, 0]
    to_band = band_blocks[0, 0]
    to_strip = strip_blocks[0, 0]
    to_summit = summit_blocks[0, 0]
    link_block = coupling[0, 0]
    lift_band = summit_band[0]
    lift_strip = summit_strip[0]
    current = (leaf_source[0, 0], band_source[0], strip_source[0], summit_source)
    for iteration in range(PASSES):
        leaf_now, band_now, strip_now, summit_now = current
        solved = leaf_forward(pair_blocks, inverses, leaf_now, reached, row_mask)
        band_term = multiply(to_band, solved, "aij,ajr->ir")
        strip_term = multiply(to_strip, solved, "aij,ajr->ir")
        summit_term = multiply(to_summit, solved, "aij,ajr->ir")
        band_partial = lax.psum(band_term, "pcol")
        band_solved = forward_block(band_inverse[0], band_now, band_partial)
        own_band = lax.dynamic_slice_in_dim(band_solved, column_place, band_slab, 0)
        summit_term = summit_term + multiply(lift_band, own_band, "ki,kn->in")
        strip_term = strip_term + multiply(link_block, band_solved, "ij,jn->in")
        strip_partial = lax.psum(strip_term, "prow")
        strip_solved = forward_block(strip_inverse[0], strip_now, strip_partial)
        own_lift = lax.dynamic_slice_in_dim(lift_strip, row_place, strip_slab, 0)
        own_strip = lax.dynamic_slice_in_dim(strip_solved, row_place, strip_slab, 0)
        summit_partial = lax.psum(
            summit_term + multiply(own_lift, own_strip, "ki,kn->in"), ("prow", "pcol")
        )
        summit_solved = forward_block(summit_inverse, summit_now, summit_partial)
        summit_answer = backward_block(
            summit_inverse, summit_solved, jnp.zeros(summit_solved.shape, jnp.float32)
        )
        strip_answer = backward_block(
            strip_inverse[0], strip_solved, multiply(lift_strip, summit_answer, "ki,in->kn")
        )
        downward = multiply(link_block, strip_answer, "ji,jn->in")
        band_piece = multiply(lift_band, summit_answer, "ki,in->kn")
        band_back = lax.psum(downward, "pcol") + lax.all_gather(
            band_piece, "pcol", axis=0, tiled=True
        )
        band_answer = backward_block(band_inverse[0], band_solved, band_back)
        outer = (
            multiply(to_band, band_answer, "aij,ir->ajr")
            + multiply(to_strip, strip_answer, "aij,ir->ajr")
            + multiply(to_summit, summit_answer, "aij,ir->ajr")
        )
        leaf_answer = leaf_backward(pair_blocks, inverses, solved, outer, reached, row_mask)
        current = (leaf_answer, band_answer, strip_answer, summit_answer)
    return (current[0][None, None], current[1][None], current[2][None], current[3])


def solution(mesh):
    placed = (
        P("prow", "pcol", None, None, None),
        P("prow", None, None),
        P("pcol", None, None),
        P(),
        P("prow", "pcol", None, None, None),
        P("prow", None, None),
        P("pcol", None, None),
        P(),
        P("prow", "pcol", None, None, None),
        P("prow", "pcol", None, None, None),
        P("prow", "pcol", None, None, None),
        P("prow", "pcol", None, None, None),
        P("prow", "pcol", None, None),
        P("prow", "pcol", None),
        P("pcol", None, None),
        P("prow", "pcol", None),
        P("prow", "pcol", None),
    )
    return jax.shard_map(
        per_device,
        mesh=mesh,
        in_specs=placed,
        out_specs=(
            P("prow", "pcol", None, None, None),
            P("prow", None, None),
            P("pcol", None, None),
            P(),
        ),
        check_vma=False,
    )
```

profile of v0, /device:TPU:2, one launch (start us, length us, event | category | flops | bytes accessed | tf_op | source)
XLA Modules:
  0.0 1181.8 jit_solution(3843605746356094015)
XLA Ops:
  14.1 1.9 constant_dynamic-update-slice_fusion.17
  15.9 2.0 constant_dynamic-update-slice_fusion.16
  17.9 2.1 constant_dynamic-update-slice_fusion.15
  20.0 2.1 constant_dynamic-update-slice_fusion.14
  22.1 2.2 constant_dynamic-update-slice_fusion.13
  25.3 2.5 constant_dynamic-update-slice_fusion.12
  28.6 2.6 constant_dynamic-update-slice_fusion.11
  31.2 2.6 constant_dynamic-update-slice_fusion.18
  33.8 2.2 convolution_bitcast_fusion.19
  42.3 2.1 convolution_bitcast_fusion.17
  44.4 2.1 convolution_bitcast_fusion.18
  46.5 84.6 %all-reduce.9.cloned.1.call-done = f32[256,128]{1,0:T(8,128)} async-done(((f32[256,128]{1,0:T(8,128)}), f32[256,128]{1,0:T(8,128)}) %all-reduce.9.cloned.1.call-update) | async-done | bytes 131088 | tf_op jit(solution)/shard_map/psum | solution.py:122
  133.0 1.7 fusion.29
  134.8 1.8 fusion.34
  136.7 105.3 %all-reduce.11.cloned.1.call-done = f32[256,128]{1,0:T(8,128)} async-done(((f32[256,128]{1,0:T(8,128)}), f32[256,128]{1,0:T(8,128)}) %all-reduce.11.cloned.1.call-update) | async-done | bytes 131088 | tf_op jit(solution)/shard_map/psum | solution.py:127
  243.8 1.8 convolution_add_fusion.8
  246.8 243.6 %all-reduce.13.cloned.1.call-done = f32[256,128]{1,0:T(8,128)} async-done(((f32[256,128]{1,0:T(8,128)}), f32[256,128]{1,0:T(8,128)}) %all-reduce.13.cloned.1.call-update) | async-done | bytes 131088 | tf_op jit(solution)/shard_map/psum | solution.py:131
  490.5 1.9 convolution_convert_fusion.8
  492.3 1.9 convolution_convert_fusion.7
  494.2 1.7 convolution_bitcast_fusion.10
  496.9 23.8 %all_gather.6 = f32[256,128]{1,0:T(8,128)} all-gather(f32[16,128]{1,0:T(8,128)S(1)} %convolution_bitcast_fusion.22), channel_id=1, replica_groups=mesh['prow'=16,'pcol'=16] {'pcol'}, dimensions={0}, use_global_device_ids=true | all-gather | bytes 139264 | tf_op jit(solution)/shard_map/all_gather | solution.py:143
  520.7 1.6 copy.39
  522.3 62.3 %all-reduce.15.cloned.1.call-done = f32[256,128]{0,1:T(8,128)} async-done(((f32[256,128]{0,1:T(8,128)}), f32[256,128]{0,1:T(8,128)}) %all-reduce.15.cloned.1.call-update) | async-done | bytes 131088 | tf_op jit(solution)/shard_map/psum | solution.py:143
  593.4 1.5 fusion.77
  594.9 2.0 constant_dynamic-update-slice_fusion.43
  596.9 2.1 constant_dynamic-update-slice_fusion.42
  599.0 2.2 constant_dynamic-update-slice_fusion.41
  601.2 2.4 constant_dynamic-update-slice_fusion.40
  603.6 2.4 constant_dynamic-update-slice_fusion.39
  606.0 2.5 constant_dynamic-update-slice_fusion.38
  608.5 2.6 constant_dynamic-update-slice_fusion.37
  611.1 2.7 constant_dynamic-update-slice_fusion.44
  613.8 2.2 convolution_bitcast_fusion.13
  616.0 2.2 convolution_bitcast_fusion.15
  618.2 2.2 convolution_bitcast_fusion.14
  620.4 89.7 %all-reduce.17.cloned.1.call-done = f32[256,128]{0,1:T(8,128)} async-done(((f32[256,128]{0,1:T(8,128)}), f32[256,128]{0,1:T(8,128)}) %all-reduce.17.cloned.1.call-update) | async-done | bytes 131088 | tf_op jit(solution)/shard_map/psum | solution.py:122
  712.0 1.8 fusion.27
  713.8 1.8 fusion.33
  715.6 105.4 %all-reduce.19.cloned.1.call-done = f32[256,128]{0,1:T(8,128)} async-done(((f32[256,128]{0,1:T(8,128)}), f32[256,128]{0,1:T(8,128)}) %all-reduce.19.cloned.1.call-update) | async-done | bytes 131088 | tf_op jit(solution)/shard_map/psum | solution.py:127
  822.8 1.8 convolution_add_fusion.6
  824.6 245.8 %all-reduce.21.cloned.1.call-done = f32[256,128]{0,1:T(8,128)} async-done(((f32[256,128]{0,1:T(8,128)}), f32[256,128]{0,1:T(8,128)}) %all-reduce.21.cloned.1.call-update) | async-done | bytes 131088 | tf_op jit(solution)/shard_map/psum | solution.py:131
  1070.4 1.9 convolution_convert_fusion.2
  1075.4 1.6 copy.44
  1077.7 22.2 %all_gather.7 = f32[256,128]{1,0:T(8,128)S(1)} all-gather(f32[16,128]{1,0:T(8,128)S(1)} %convolution_bitcast_fusion.21), channel_id=1, replica_groups=mesh['prow'=16,'pcol'=16] {'pcol'}, dimensions={0}, use_global_device_ids=true | all-gather | bytes 139264 | tf_op jit(solution)/shard_map/all_gather | solution.py:143
  1100.7 62.5 %all-reduce.23.cloned.1.call-done = f32[256,128]{0,1:T(8,128)} async-done(((f32[256,128]{0,1:T(8,128)}), f32[256,128]{0,1:T(8,128)}) %all-reduce.23.cloned.1.call-update) | async-done | bytes 131088 | tf_op jit(solution)/shard_map/psum | solution.py:143
  1164.4 1.3 fusion.130
  1166.4 1.7 convolution_add_fusion.1
  1171.9 2.0 fusion.121
  (269 shorter events, 42.9 us)
Async XLA Ops:
  7.2 26.6 %copy-start = (bf16[1,1,8,256,256]{4,3,2,1,0:T(8,128)(2,1)S(1)}, bf16[1,1,8,256,256]{4,3,2,1,0:T(8,128)(2,1)}, u32[]{:S(2)}) copy-start(bf16[1,1,8,256,256]{4,3,2,1,0:T(8,128)(2,1)} %param.54) | copy-start | bytes 3145732
  7.2 124.0 %all-reduce.9.cloned.1.call-start = ((), (), s32[]{:S(2)}) async-start(), calls=%async_computation | async-start | bytes 262144 | tf_op jit(solution)/shard_map/psum | solution.py:122
  10.6 20.6 %copy-start.79 = (bf16[7]{0:T(256)(128)(2,1)}, bf16[7]{0:T(256)(128)(2,1)S(1)}, u32[]{:S(2)}) copy-start(bf16[7]{0:T(256)(128)(2,1)S(1)} %fusion.590) | copy-start | bytes 46
  10.6 18.0 %copy-start.80 = (bf16[6]{0:T(256)(128)(2,1)}, bf16[6]{0:T(256)(128)(2,1)S(1)}, u32[]{:S(2)}) copy-start(bf16[6]{0:T(256)(128)(2,1)S(1)} %fusion.589) | copy-start | bytes 40
  10.6 14.7 %copy-start.81 = (bf16[5]{0:T(256)(128)(2,1)}, bf16[5]{0:T(256)(128)(2,1)S(1)}, u32[]{:S(2)}) copy-start(bf16[5]{0:T(256)(128)(2,1)S(1)} %fusion.588) | copy-start | bytes 34
  10.7 13.6 %copy-start.82 = (bf16[4]{0:T(256)(128)(2,1)}, bf16[4]{0:T(256)(128)(2,1)S(1)}, u32[]{:S(2)}) copy-start(bf16[4]{0:T(256)(128)(2,1)S(1)} %fusion.587) | copy-start | bytes 28
  10.7 13.6 %copy-start.83 = (bf16[3]{0:T(256)(128)(2,1)}, bf16[3]{0:T(256)(128)(2,1)S(1)}, u32[]{:S(2)}) copy-start(bf16[3]{0:T(256)(128)(2,1)S(1)} %fusion.586) | copy-start | bytes 22
  10.7 13.6 %copy-start.84 = (bf16[2]{0:T(256)(128)(2,1)}, bf16[2]{0:T(256)(128)(2,1)S(1)}, u32[]{:S(2)}) copy-start(bf16[2]{0:T(256)(128)(2,1)S(1)} %fusion.585) | copy-start | bytes 16
  12.1 12.2 %copy-start.45 = (f32[1,256]{1,0:T(1,128)}, f32[1,256]{1,0:T(1,128)S(1)}, u32[]{:S(2)}) copy-start(f32[1,256]{1,0:T(1,128)S(1)} %get-tuple-element.241) | copy-start | bytes 3076
  12.2 12.2 %copy-start.48 = (f32[1,256]{1,0:T(1,128)}, f32[1,256]{1,0:T(1,128)S(1)}, u32[]{:S(2)}) copy-start(f32[1,256]{1,0:T(1,128)S(1)} %get-tuple-element.240) | copy-start | bytes 3076
  12.2 12.2 %copy-start.61 = (f32[1,256]{1,0:T(1,128)}, f32[1,256]{1,0:T(1,128)S(1)}, u32[]{:S(2)}) copy-start(f32[1,256]{1,0:T(1,128)S(1)} %get-tuple-element.244) | copy-start | bytes 3076
  12.2 13.1 %copy-start.51 = (f32[1,256]{1,0:T(1,128)}, f32[1,256]{1,0:T(1,128)S(1)}, u32[]{:S(2)}) copy-start(f32[1,256]{1,0:T(1,128)S(1)} %get-tuple-element.239) | copy-start | bytes 3076
  12.2 16.4 %copy-start.54 = (f32[1,256]{1,0:T(1,128)}, f32[1,256]{1,0:T(1,128)S(1)}, u32[]{:S(2)}) copy-start(f32[1,256]{1,0:T(1,128)S(1)} %get-tuple-element.238) | copy-start | bytes 3076
  12.2 19.0 %copy-start.57 = (f32[1,256]{1,0:T(1,128)}, f32[1,256]{1,0:T(1,128)S(1)}, u32[]{:S(2)}) copy-start(f32[1,256]{1,0:T(1,128)S(1)} %get-tuple-element.237) | copy-start | bytes 3076
  15.9 11.8 %copy-start.26 = (bf16[128,256]{1,0:T(8,128)(2,1)}, bf16[128,256]{1,0:T(8,128)(2,1)S(1)}, u32[]{:S(2)}) copy-start(bf16[128,256]{1,0:T(8,128)(2,1)S(1)} %get-tuple-element.245) | copy-start | bytes 196612
  17.9 9.9 copy-start.28
  20.0 7.8 copy-start.31
  22.1 5.7 copy-start.34
  25.3 17.0 %copy-start.2 = (bf16[1,1,8,256,256]{4,3,2,1,0:T(8,128)(2,1)S(1)}, bf16[1,1,8,256,256]{4,3,2,1,0:T(8,128)(2,1)}, u32[]{:S(2)}) copy-start(bf16[1,1,8,256,256]{4,3,2,1,0:T(8,128)(2,1)} %param.56) | copy-start | bytes 3145732
  28.6 15.8 %copy-start.1 = (bf16[1,1,8,256,256]{4,3,2,1,0:T(8,128)(2,1)S(1)}, bf16[1,1,8,256,256]{4,3,2,1,0:T(8,128)(2,1)}, u32[]{:S(2)}) copy-start(bf16[1,1,8,256,256]{4,3,2,1,0:T(8,128)(2,1)} %param.55) | copy-start | bytes 3145732
  31.2 101.8 %copy-start.9 = (bf16[1,1,256,256]{3,2,1,0:T(8,128)(2,1)S(1)}, bf16[1,1,256,256]{3,2,1,0:T(8,128)(2,1)}, u32[]{:S(2)}) copy-start(bf16[1,1,256,256]{3,2,1,0:T(8,128)(2,1)} %param.57) | copy-start | bytes 393220
  33.8 101.0 %copy-start.25 = (bf16[1,16,256]{2,1,0:T(8,128)(2,1)S(1)}, bf16[1,16,256]{2,1,0:T(8,128)(2,1)}, u32[]{:S(2)}) copy-start(bf16[1,16,256]{2,1,0:T(8,128)(2,1)} %param.58) | copy-start | bytes 24580
  33.8 208.2 %copy-start.8 = (bf16[1,256,256]{2,1,0:T(8,128)(2,1)S(1)}, bf16[1,256,256]{2,1,0:T(8,128)(2,1)}, u32[]{:S(2)}) copy-start(bf16[1,256,256]{2,1,0:T(8,128)(2,1)} %param.51) | copy-start | bytes 393220
  33.8 456.7 %copy-start.10 = (bf16[256,256]{1,0:T(8,128)(2,1)S(1)}, bf16[256,256]{1,0:T(8,128)(2,1)}, u32[]{:S(2)}) copy-start(bf16[256,256]{1,0:T(8,128)(2,1)} %param.52) | copy-start | bytes 393220
  36.0 206.0 %all-reduce.11.cloned.1.call-start = ((), (), s32[]{:S(2)}) async-start(), calls=%async_computation.1 | async-start | bytes 262144 | tf_op jit(solution)/shard_map/psum | solution.py:127
  134.8 355.7 %all-reduce.13.cloned.1.call-start = ((), (), s32[]{:S(2)}) async-start(), calls=%async_computation.2 | async-start | bytes 262144 | tf_op jit(solution)/shard_map/psum | solution.py:131
  245.6 339.0 %all-reduce.15.cloned.1.call-start = ((), (), s32[]{:S(2)}) async-start(), calls=%async_computation.3 | async-start | bytes 262144 | tf_op jit(solution)/shard_map/psum | solution.py:143
  495.9 214.2 %all-reduce.17.cloned.1.call-start = ((), (), s32[]{:S(2)}) async-start(), calls=%async_computation.4 | async-start | bytes 262144 | tf_op jit(solution)/shard_map/psum | solution.py:122
  584.6 3.6 copy-start.12
  586.8 2.4 copy-start.3
  586.9 2.4 copy-start.70
  588.5 1.9 copy-start.38
  588.6 2.0 copy-start.68
  589.8 2.4 copy-start.32
  590.4 1.9 copy-start.72
  590.4 2.2 copy-start.29
  590.6 2.2 copy-start.19
  590.6 2.8 copy-start.27
  590.6 2.8 copy-start.62
  618.2 202.9 %all-reduce.19.cloned.1.call-start = ((), (), s32[]{:S(2)}) async-start(), calls=%async_computation.5 | async-start | bytes 262144 | tf_op jit(solution)/shard_map/psum | solution.py:127
  713.8 356.7 %all-reduce.21.cloned.1.call-start = ((), (), s32[]{:S(2)}) async-start(), calls=%async_computation.6 | async-start | bytes 262144 | tf_op jit(solution)/shard_map/psum | solution.py:131
  824.6 338.6 %all-reduce.23.cloned.1.call-start = ((), (), s32[]{:S(2)}) async-start(), calls=%async_computation.7 | async-start | bytes 262144 | tf_op jit(solution)/shard_map/psum | solution.py:143
  1073.5 94.6 %copy-start.11 = (bf16[128,256]{1,0:T(8,128)(2,1)S(1)}, bf16[128,256]{1,0:T(8,128)(2,1)}, u32[]{:S(2)}) copy-start(bf16[128,256]{1,0:T(8,128)(2,1)} %convolution_convert_fusion.2) | copy-start | bytes 196612
  1165.7 2.8 copy-start.44
  1165.7 2.8 copy-start.59
  1165.7 3.0 copy-start.71
  1166.4 2.1 copy-start.7
  1166.4 2.7 copy-start.4
  (45 other events, 60.7 us)
Sparse Core Ops, SparseCore 0:
  36.1 94.9 all-reduce.8
  134.9 107.0 all-reduce.10
  248.1 242.3 all-reduce.12
  496.0 88.5 all-reduce.14
  618.3 91.8 all-reduce.16
  713.9 107.1 all-reduce.18
  828.0 242.3 all-reduce.20
  1074.5 88.5 all-reduce.22
where the time goes:
time: 1180 us
  waiting for transfers between devices  999 us (85%)
  matrix products  92.7 us (8%)
  blocking collectives  46 us (4%)
  local copies, waits for them, and re-layouts  23.6 us (2%)
  between operations  16.2 us (1%)
    psum x2, waiting for transfers between devices, per_device(): lax.psum(summit_term + multiply(own_lift, own_strip, 'ki,kn->in'), ('prow...  489 us
    psum x2, waiting for transfers between devices, per_device(): strip_partial = lax.psum(strip_term, 'prow')  211 us
    psum x2, waiting for transfers between devices, per_device(): band_partial = lax.psum(band_term, 'pcol')  174 us
    psum x2, waiting for transfers between devices, per_device(): lax.psum(downward, 'pcol')  125 us
    dot_general x76, matrix products, multiply(): return jnp.einsum(form, left, right, preferred_element_type=jnp.float32)  92.7 us
    all_gather x2, blocking collectives, per_device(): lax.all_gather(band_piece, 'pcol', axis=0, tiled=True)  46 us
  transfers between devices with their start and end apart: 8, of which 8 were waited for; matrix products, arithmetic and copies ran while one was open for 2% of the time, Pallas kernels for 0%

commit v1 on v0

--- a/solution.py
+++ b/solution.py
@@ -119,7 +119,11 @@
         band_term = multiply(to_band, solved, "aij,ajr->ir")
         strip_term = multiply(to_strip, solved, "aij,ajr->ir")
         summit_term = multiply(to_summit, solved, "aij,ajr->ir")
-        band_partial = lax.psum(band_term, "pcol")
+        band_partial = band_term
+        for hop in (1, 2, 4, 8):
+            band_partial = band_partial + lax.ppermute(
+                band_partial, "pcol", [(dev, dev ^ hop) for dev in range(16)]
+            )
         band_solved = forward_block(band_inverse[0], band_now, band_partial)
         own_band = lax.dynamic_slice_in_dim(band_solved, column_place, band_slab, 0)
         summit_term = summit_term + multiply(lift_band, own_band, "ki,kn->in")

time: 1180 us -> 1040 us (0.88)
  waiting for transfers between devices: 999 us -> 853 us
  starting transfers between devices: 0.33 us -> 12.5 us
    psum x2 -> x0, waiting for transfers between devices: 174 us -> none  [per_device(): band_partial = lax.psum(band_term, 'pcol')]
    ppermute x0 -> x8, waiting for transfers between devices: none -> 24.7 us  [per_device(): lax.ppermute(band_partial, 'pcol', [(dev, dev ^ hop) for dev in range(16)])]
    ppermute x0 -> x8, starting transfers between devices: none -> 12.2 us  [per_device(): lax.ppermute(band_partial, 'pcol', [(dev, dev ^ hop) for dev in range(16)])]
  transfers between devices with their start and end apart: 8 -> 14, of which waited for: 8 -> 13; matrix products, arithmetic and copies ran while one was open for 2% -> 2% of each run, Pallas kernels for 0% -> 0%
where the time goes in v1:
time: 1040 us
  waiting for transfers between devices  853 us (82%)
  matrix products  85.8 us (8%)
  blocking collectives  46.2 us (4%)
  local copies, waits for them, and re-layouts  23.3 us (2%)
  between operations  16.2 us (2%)
  starting transfers between devices  12.5 us (1%)
    psum x2, waiting for transfers between devices, per_device(): lax.psum(summit_term + multiply(own_lift, own_strip, 'ki,kn->in'), ('prow...  490 us
    psum x2, waiting for transfers between devices, per_device(): strip_partial = lax.psum(strip_term, 'prow')  214 us
    psum x2, waiting for transfers between devices, per_device(): lax.psum(downward, 'pcol')  125 us
    dot_general x76, matrix products, multiply(): return jnp.einsum(form, left, right, preferred_element_type=jnp.float32)  85.8 us
    all_gather x2, blocking collectives, per_device(): lax.all_gather(band_piece, 'pcol', axis=0, tiled=True)  46.2 us
    ppermute x8, waiting for transfers between devices, per_device(): lax.ppermute(band_partial, 'pcol', [(dev, dev ^ hop) for dev in range(16)])  24.7 us
  transfers between devices with their start and end apart: 14, of which 13 were waited for; matrix products, arithmetic and copies ran while one was open for 2% of the time, Pallas kernels for 0%

profile of v1, /device:TPU:2, one launch (start us, length us, event | category | flops | bytes accessed | tf_op | source)
XLA Modules:
  0.0 1042.0 jit_solution(14149702212234950948)
XLA Ops:
  14.0 1.9 constant_dynamic-update-slice_fusion.17
  15.9 2.0 constant_dynamic-update-slice_fusion.16
  17.9 2.1 constant_dynamic-update-slice_fusion.15
  20.0 2.1 constant_dynamic-update-slice_fusion.14
  22.1 2.2 constant_dynamic-update-slice_fusion.13
  24.5 2.3 constant_dynamic-update-slice_fusion.12
  26.8 2.6 constant_dynamic-update-slice_fusion.11
  29.4 2.7 constant_dynamic-update-slice_fusion.18
  32.1 2.2 convolution_bitcast_fusion.19
  43.3 3.0 collective-permute-start.1
  47.5 2.3 collective-permute-done.1
  50.7 2.1 convolution_bitcast_fusion.17
  52.8 2.1 collective-permute-done.2
  55.0 3.0 collective-permute-start.3
  59.4 2.1 collective-permute-done.3
  63.3 1.8 fusion.34
  65.1 108.8 %all-reduce.7.cloned.1.call-done = f32[256,128]{1,0:T(8,128)} async-done(((f32[256,128]{1,0:T(8,128)}), f32[256,128]{1,0:T(8,128)}) %all-reduce.7.cloned.1.call-update) | async-done | bytes 131088 | tf_op jit(solution)/shard_map/psum | solution.py:131
  175.6 1.8 convolution_add_fusion.8
  178.7 244.6 %all-reduce.9.cloned.1.call-done = f32[256,128]{1,0:T(8,128)} async-done(((f32[256,128]{1,0:T(8,128)}), f32[256,128]{1,0:T(8,128)}) %all-reduce.9.cloned.1.call-update) | async-done | bytes 131088 | tf_op jit(solution)/shard_map/psum | solution.py:135
  423.3 1.9 convolution_convert_fusion.8
  425.1 1.9 convolution_convert_fusion.7
  427.0 1.7 convolution_bitcast_fusion.10
  429.7 23.9 %all_gather.6 = f32[256,128]{1,0:T(8,128)} all-gather(f32[16,128]{1,0:T(8,128)S(1)} %convolution_bitcast_fusion.22), channel_id=1, replica_groups=mesh['prow'=16,'pcol'=16] {'pcol'}, dimensions={0}, use_global_device_ids=true | all-gather | bytes 139264 | tf_op jit(solution)/shard_map/all_gather | solution.py:147
  453.6 1.7 copy.41
  455.3 62.2 %all-reduce.11.cloned.1.call-done = f32[256,128]{0,1:T(8,128)} async-done(((f32[256,128]{0,1:T(8,128)}), f32[256,128]{0,1:T(8,128)}) %all-reduce.11.cloned.1.call-update) | async-done | bytes 131088 | tf_op jit(solution)/shard_map/psum | solution.py:147
  527.6 2.0 constant_dynamic-update-slice_fusion.43
  529.6 2.1 constant_dynamic-update-slice_fusion.42
  531.7 2.2 constant_dynamic-update-slice_fusion.41
  533.9 2.4 constant_dynamic-update-slice_fusion.40
  536.3 2.4 constant_dynamic-update-slice_fusion.39
  538.7 2.5 constant_dynamic-update-slice_fusion.38
  541.2 2.6 constant_dynamic-update-slice_fusion.37
  543.8 2.7 constant_dynamic-update-slice_fusion.44
  548.5 4.8 collective-permute-done.4
  554.8 5.1 collective-permute-done.5
  560.7 2.2 convolution_bitcast_fusion.13
  562.9 3.4 collective-permute-done.6
  568.0 4.8 collective-permute-done.7
  574.6 1.8 fusion.33
  576.4 105.1 %all-reduce.13.cloned.1.call-done = f32[256,128]{0,1:T(8,128)} async-done(((f32[256,128]{0,1:T(8,128)}), f32[256,128]{0,1:T(8,128)}) %all-reduce.13.cloned.1.call-update) | async-done | bytes 131088 | tf_op jit(solution)/shard_map/psum | solution.py:131
  683.3 1.8 convolution_add_fusion.6
  685.1 245.6 %all-reduce.15.cloned.1.call-done = f32[256,128]{0,1:T(8,128)} async-done(((f32[256,128]{0,1:T(8,128)}), f32[256,128]{0,1:T(8,128)}) %all-reduce.15.cloned.1.call-update) | async-done | bytes 131088 | tf_op jit(solution)/shard_map/psum | solution.py:135
  930.7 1.9 convolution_convert_fusion.2
  935.7 1.6 copy.46
  938.0 22.3 %all_gather.7 = f32[256,128]{1,0:T(8,128)S(1)} all-gather(f32[16,128]{1,0:T(8,128)S(1)} %convolution_bitcast_fusion.21), channel_id=1, replica_groups=mesh['prow'=16,'pcol'=16] {'pcol'}, dimensions={0}, use_global_device_ids=true | all-gather | bytes 139264 | tf_op jit(solution)/shard_map/all_gather | solution.py:147
  961.0 62.4 %all-reduce.17.cloned.1.call-done = f32[256,128]{0,1:T(8,128)} async-done(((f32[256,128]{0,1:T(8,128)}), f32[256,128]{0,1:T(8,128)}) %all-reduce.17.cloned.1.call-update) | async-done | bytes 131088 | tf_op jit(solution)/shard_map/psum | solution.py:147
  1026.7 1.7 convolution_add_fusion.1
  1032.2 1.9 fusion.121
  (292 shorter events, 55.7 us)
Async XLA Ops:
  7.2 24.9 %copy-start = (bf16[1,1,8,256,256]{4,3,2,1,0:T(8,128)(2,1)S(1)}, bf16[1,1,8,256,256]{4,3,2,1,0:T(8,128)(2,1)}, u32[]{:S(2)}) copy-start(bf16[1,1,8,256,256]{4,3,2,1,0:T(8,128)(2,1)} %param.54) | copy-start | bytes 3145732
  7.2 12.8 %copy-start.6 = (bf16[1,1,8,256,256]{4,3,2,1,0:T(8,128)(2,1)S(1)}, bf16[1,1,8,256,256]{4,3,2,1,0:T(8,128)(2,1)}, u32[]{:S(2)}) copy-start(bf16[1,1,8,256,256]{4,3,2,1,0:T(8,128)(2,1)} %param.49) | copy-start | bytes 3145732
  7.2 166.7 %all-reduce.7.cloned.1.call-start = ((), (), s32[]{:S(2)}) async-start(), calls=%async_computation | async-start | bytes 262144 | tf_op jit(solution)/shard_map/psum | solution.py:131
  10.6 18.8 %copy-start.82 = (bf16[7]{0:T(256)(128)(2,1)}, bf16[7]{0:T(256)(128)(2,1)S(1)}, u32[]{:S(2)}) copy-start(bf16[7]{0:T(256)(128)(2,1)S(1)} %fusion.590) | copy-start | bytes 46
  10.6 16.2 %copy-start.83 = (bf16[6]{0:T(256)(128)(2,1)}, bf16[6]{0:T(256)(128)(2,1)S(1)}, u32[]{:S(2)}) copy-start(bf16[6]{0:T(256)(128)(2,1)S(1)} %fusion.589) | copy-start | bytes 40
  10.6 13.8 %copy-start.84 = (bf16[5]{0:T(256)(128)(2,1)}, bf16[5]{0:T(256)(128)(2,1)S(1)}, u32[]{:S(2)}) copy-start(bf16[5]{0:T(256)(128)(2,1)S(1)} %fusion.588) | copy-start | bytes 34
  10.7 13.7 %copy-start.85 = (bf16[4]{0:T(256)(128)(2,1)}, bf16[4]{0:T(256)(128)(2,1)S(1)}, u32[]{:S(2)}) copy-start(bf16[4]{0:T(256)(128)(2,1)S(1)} %fusion.587) | copy-start | bytes 28
  10.7 13.7 %copy-start.86 = (bf16[3]{0:T(256)(128)(2,1)}, bf16[3]{0:T(256)(128)(2,1)S(1)}, u32[]{:S(2)}) copy-start(bf16[3]{0:T(256)(128)(2,1)S(1)} %fusion.586) | copy-start | bytes 22
  10.7 13.7 %copy-start.87 = (bf16[2]{0:T(256)(128)(2,1)}, bf16[2]{0:T(256)(128)(2,1)S(1)}, u32[]{:S(2)}) copy-start(bf16[2]{0:T(256)(128)(2,1)S(1)} %fusion.585) | copy-start | bytes 16
  12.1 12.3 %copy-start.50 = (f32[1,256]{1,0:T(1,128)}, f32[1,256]{1,0:T(1,128)S(1)}, u32[]{:S(2)}) copy-start(f32[1,256]{1,0:T(1,128)S(1)} %get-tuple-element.241) | copy-start | bytes 3076
  12.1 12.3 %copy-start.53 = (f32[1,256]{1,0:T(1,128)}, f32[1,256]{1,0:T(1,128)S(1)}, u32[]{:S(2)}) copy-start(f32[1,256]{1,0:T(1,128)S(1)} %get-tuple-element.240) | copy-start | bytes 3076
  12.1 12.3 %copy-start.66 = (f32[1,256]{1,0:T(1,128)}, f32[1,256]{1,0:T(1,128)S(1)}, u32[]{:S(2)}) copy-start(f32[1,256]{1,0:T(1,128)S(1)} %get-tuple-element.244) | copy-start | bytes 3076
  12.1 12.3 %copy-start.56 = (f32[1,256]{1,0:T(1,128)}, f32[1,256]{1,0:T(1,128)S(1)}, u32[]{:S(2)}) copy-start(f32[1,256]{1,0:T(1,128)S(1)} %get-tuple-element.239) | copy-start | bytes 3076
  12.1 14.7 %copy-start.59 = (f32[1,256]{1,0:T(1,128)}, f32[1,256]{1,0:T(1,128)S(1)}, u32[]{:S(2)}) copy-start(f32[1,256]{1,0:T(1,128)S(1)} %get-tuple-element.238) | copy-start | bytes 3076
  12.1 17.3 %copy-start.62 = (f32[1,256]{1,0:T(1,128)}, f32[1,256]{1,0:T(1,128)S(1)}, u32[]{:S(2)}) copy-start(f32[1,256]{1,0:T(1,128)S(1)} %get-tuple-element.237) | copy-start | bytes 3076
  15.9 8.5 copy-start.31
  17.9 6.5 copy-start.33
  20.0 4.5 copy-start.36
  26.8 23.9 %copy-start.2 = (bf16[1,1,8,256,256]{4,3,2,1,0:T(8,128)(2,1)S(1)}, bf16[1,1,8,256,256]{4,3,2,1,0:T(8,128)(2,1)}, u32[]{:S(2)}) copy-start(bf16[1,1,8,256,256]{4,3,2,1,0:T(8,128)(2,1)} %param.56) | copy-start | bytes 3145732
  29.4 28.6 %copy-start.1 = (bf16[1,1,8,256,256]{4,3,2,1,0:T(8,128)(2,1)S(1)}, bf16[1,1,8,256,256]{4,3,2,1,0:T(8,128)(2,1)}, u32[]{:S(2)}) copy-start(bf16[1,1,8,256,256]{4,3,2,1,0:T(8,128)(2,1)} %param.55) | copy-start | bytes 3145732
  32.1 30.3 %copy-start.10 = (bf16[1,1,256,256]{3,2,1,0:T(8,128)(2,1)S(1)}, bf16[1,1,256,256]{3,2,1,0:T(8,128)(2,1)}, u32[]{:S(2)}) copy-start(bf16[1,1,256,256]{3,2,1,0:T(8,128)(2,1)} %param.57) | copy-start | bytes 393220
  32.1 31.2 %copy-start.30 = (bf16[1,16,256]{2,1,0:T(8,128)(2,1)S(1)}, bf16[1,16,256]{2,1,0:T(8,128)(2,1)}, u32[]{:S(2)}) copy-start(bf16[1,16,256]{2,1,0:T(8,128)(2,1)} %param.58) | copy-start | bytes 24580
  32.1 141.8 %copy-start.9 = (bf16[1,256,256]{2,1,0:T(8,128)(2,1)S(1)}, bf16[1,256,256]{2,1,0:T(8,128)(2,1)}, u32[]{:S(2)}) copy-start(bf16[1,256,256]{2,1,0:T(8,128)(2,1)} %param.51) | copy-start | bytes 393220
  34.3 389.0 %copy-start.11 = (bf16[256,256]{1,0:T(8,128)(2,1)S(1)}, bf16[256,256]{1,0:T(8,128)(2,1)}, u32[]{:S(2)}) copy-start(bf16[256,256]{1,0:T(8,128)(2,1)} %param.52) | copy-start | bytes 393220
  34.3 8.0 collective-permute-start
  41.1 20.4 %copy-start.12 = (bf16[1,256,256]{2,1,0:T(8,128)(2,1)S(1)}, bf16[1,256,256]{2,1,0:T(8,128)(2,1)}, u32[]{:S(2)}) copy-start(bf16[1,256,256]{2,1,0:T(8,128)(2,1)} %param.50) | copy-start | bytes 393220
  41.1 20.4 %copy-start.28 = (bf16[1,256,128]{1,2,0:T(8,128)(2,1)S(1)}, bf16[1,256,128]{1,2,0:T(8,128)(2,1)}, u32[]{:S(2)}) copy-start(bf16[1,256,128]{1,2,0:T(8,128)(2,1)} %copy.33) | copy-start | bytes 196612
  43.3 6.6 collective-permute-start.1
  49.9 5.1 collective-permute-start.2
  55.0 6.6 collective-permute-start.3
  63.2 360.1 %all-reduce.9.cloned.1.call-start = ((), (), s32[]{:S(2)}) async-start(), calls=%async_computation.1 | async-start | bytes 262144 | tf_op jit(solution)/shard_map/psum | solution.py:135
  177.5 340.0 %all-reduce.11.cloned.1.call-start = ((), (), s32[]{:S(2)}) async-start(), calls=%async_computation.2 | async-start | bytes 262144 | tf_op jit(solution)/shard_map/psum | solution.py:147
  428.7 252.8 %all-reduce.13.cloned.1.call-start = ((), (), s32[]{:S(2)}) async-start(), calls=%async_computation.3 | async-start | bytes 262144 | tf_op jit(solution)/shard_map/psum | solution.py:131
  517.4 3.6 copy-start.15
  523.4 2.8 copy-start.32
  546.5 21.0 %copy-start.5 = (bf16[8,256,128]{1,2,0:T(8,128)(2,1)S(1)}, bf16[8,256,128]{1,2,0:T(8,128)(2,1)}, u32[]{:S(2)}) copy-start(bf16[8,256,128]{1,2,0:T(8,128)(2,1)} %get-tuple-element.261) | copy-start | bytes 1572868
  546.5 26.3 %copy-start.13 = (bf16[1,256,256]{2,1,0:T(8,128)(2,1)S(1)}, bf16[1,256,256]{2,1,0:T(8,128)(2,1)}, u32[]{:S(2)}) copy-start(bf16[1,256,256]{2,1,0:T(8,128)(2,1)} %param.50) | copy-start | bytes 393220
  546.5 26.3 %copy-start.19 = (bf16[128,256]{1,0:T(8,128)(2,1)S(1)}, bf16[128,256]{1,0:T(8,128)(2,1)}, u32[]{:S(2)}) copy-start(bf16[128,256]{1,0:T(8,128)(2,1)} %copy-done.18) | copy-start | bytes 196612
  548.1 5.2 collective-permute-start.4
  553.3 6.6 collective-permute-start.5
  559.9 6.3 collective-permute-start.6
  566.3 6.6 collective-permute-start.7
  574.5 356.2 %all-reduce.15.cloned.1.call-start = ((), (), s32[]{:S(2)}) async-start(), calls=%async_computation.4 | async-start | bytes 262144 | tf_op jit(solution)/shard_map/psum | solution.py:135
  685.1 338.4 %all-reduce.17.cloned.1.call-start = ((), (), s32[]{:S(2)}) async-start(), calls=%async_computation.5 | async-start | bytes 262144 | tf_op jit(solution)/shard_map/psum | solution.py:147
  933.9 94.5 %copy-start.14 = (bf16[128,256]{1,0:T(8,128)(2,1)S(1)}, bf16[128,256]{1,0:T(8,128)(2,1)}, u32[]{:S(2)}) copy-start(bf16[128,256]{1,0:T(8,128)(2,1)} %convolution_convert_fusion.2) | copy-start | bytes 196612
  1025.9 2.8 copy-start.49
  1025.9 2.8 copy-start.64
  1026.0 3.0 copy-start.76
  (54 other events, 85.1 us)
Sparse Core Ops, SparseCore 0:
  63.3 110.5 all-reduce.6
  180.9 242.3 all-reduce.8
  428.8 88.5 all-reduce.10
  574.6 106.8 all-reduce.12
  688.3 242.3 all-reduce.14
  934.8 88.5 all-reduce.16
